TPU v7x, 256 devices: a whole 4x4x8 slice. The times are simulated.
256 devices in a mesh: fsdp: 32 (over y, z), tp: 8 (over x, core).
Axes of the slice: x: 4, y: 4, z: 8, core: 2. Of those that a mesh axis runs over, the one named last changes fastest.
Arguments:
- hidden: bfloat16 [4096, 14336], P('fsdp', 'tp'), may hold values from -6 to 6
- residual: bfloat16 [4096, 8192], P('tp', 'fsdp'), may hold values from -22 to 22
- target: bfloat16 [4096, 8192], P('tp', 'fsdp'), may hold values from -8.2 to 8.2
- norm_gain: float32 [8192], P('fsdp'), may hold values from 0.1 to 1.9
- weight: bfloat16 [14336, 8192], P('tp', 'fsdp'), may hold values from -0.03775065 to 0.03775065
- v_prev: float32 [14336, 8192], P('tp', 'fsdp'), may hold values from -6 to 6
- v_cur: float32 [14336, 8192], P('tp', 'fsdp'), may hold values from -6.3 to 6.3
- beta_prev: float32 [], replicated, may hold values from 0.125 to 0.375
Outputs:
- v_next: float32 [14336, 8192], P('tp', 'fsdp')
- alpha: float32 [], replicated
- beta: float32 [], replicated
All inputs are finite; a program needn't handle non-finite values.
Results may differ from a plain program's by a relative error of at most 0.0047.
Values may be sent and summed in bfloat16 or wider, within the bound.
A program may use at most 128 MiB of HBM per device.

v0:
```python
import jax
import jax.numpy as jnp
from jax import lax
from jax.sharding import PartitionSpec as P

D = 8192
FF = 14336


EPSILON = 1e-05


def on_device(hidden, residual, target, norm_gain, weight, v_prev, v_cur, beta_prev):
    columns = weight.shape[1]
    stacked = jnp.concatenate([weight, v_cur.astype(jnp.bfloat16)], axis=1)
    gathered = lax.all_gather(hidden, "fsdp", axis=0, tiled=True)
    total_rows = gathered.shape[0]
    block_rows = gathered
    sums = lax.psum_scatter(
        jnp.dot(block_rows, stacked, preferred_element_type=jnp.float32),
        "tp",
        scatter_dimension=0,
        tiled=True,
    )
    resid_rows, target_rows = (residual, target)
    outputs = resid_rows.astype(jnp.float32) + sums[:, :columns]
    tangent = sums[:, columns:]
    target_f = target_rows.astype(jnp.float32)
    gain_sq = norm_gain * norm_gain
    squares = lax.psum(jnp.sum(outputs * outputs, axis=1), "fsdp")
    radius = jnp.sqrt(squares[:, None] / D + EPSILON)
    normed = outputs / radius
    adjoint = norm_gain * (norm_gain * normed - target_f)
    along_adj, along_tan = lax.psum(
        (jnp.sum(normed * adjoint, axis=1), jnp.sum(normed * tangent, axis=1)), "fsdp"
    )
    centre = along_adj[:, None] / D
    stretch = along_tan[:, None] / D
    normed_dot = (tangent - normed * stretch) / radius
    adjoint_dot = gain_sq * normed_dot
    slope = lax.psum(jnp.sum(normed_dot * adjoint + normed * adjoint_dot, axis=1), "fsdp")
    centre_dot = slope[:, None] / D
    hessian_rows = (
        adjoint_dot
        - normed_dot * centre
        - normed * centre_dot
        - (adjoint - normed * centre) * (stretch / radius)
    ) / (total_rows * radius)
    hessian_rows = hessian_rows.astype(jnp.bfloat16)
    block_rows = gathered
    product = lax.dot_general(
        block_rows,
        lax.all_gather(hessian_rows, "tp", axis=0, tiled=True),
        (((0,), (0,)), ((), ())),
        preferred_element_type=jnp.float32,
    )
    scale = 1.0 / (FF * D)
    update = product - beta_prev * v_prev
    alpha = lax.psum(jnp.sum(update * v_cur), ("fsdp", "tp")) * scale
    update = update - alpha * v_cur
    beta = jnp.sqrt(lax.psum(jnp.sum(update * update), ("fsdp", "tp")) * scale)
    return (update / beta, alpha, beta)


def solution(mesh):
    return jax.shard_map(
        on_device,
        mesh=mesh,
        in_specs=(
            P("fsdp", "tp"),
            P("tp", "fsdp"),
            P("tp", "fsdp"),
            P("fsdp"),
            P("tp", "fsdp"),
            P("tp", "fsdp"),
            P("tp", "fsdp"),
            P(),
        ),
        out_specs=(P("tp", "fsdp"), P(), P()),
        check_vma=False,
    )
```

profile of v0, /device:TPU:1, one launch (start us, length us, event | category | flops | bytes accessed | tf_op | source)
XLA Modules:
  0.0 630.7 jit_solution(17872438816340499073)
XLA Ops:
  7.2 0.0 copy-start.4
  7.2 0.0 all-gather.3.cloned.1.call-start
  7.2 0.7 all-gather.3.cloned.1.call-update
  7.9 0.0 reduce-scatter.2.cloned.1.call-start
  8.0 1.6 convert_element_type.12
  9.5 134.5 %all-gather.3.cloned.1.call-done = bf16[4096,1792]{1,0:T(8,128)(2,1)} async-done(((bf16[128,1792]{1,0:T(8,128)(2,1)}), bf16[4096,1792]{1,0:T(8,128)(2,1)}) %all-gather.3.cloned.1.call-update) | async-done | bytes 14680080 | tf_op jit(solution)/shard_map/all_gather | solution.py:16
  144.1 0.0 copy-done.4
  144.1 13.1 %convolution_bitcast_fusion = f32[4096,512]{0,1:T(8,128)} fusion(bf16[4096,1792]{1,0:T(8,128)(2,1)} %all-gather.3.cloned.1.call-done, bf16[1792,256]{1,0:T(8,128)(2,1)S(1)} %convert_element_type.12, bf16[1792,256]{1,0:T(8,128)(2,1)S(1)} %copy-done.4), kind=kOutput, calls=%fused_computation | convolution fusion | flops 7519862784 | bytes 24903680 | tf_op jit(solution)/shard_map/dot_general | solution.py:20
  157.2 0.0 copy-start.1
  157.2 0.0 copy-start.2
  157.2 0.0 copy-start.3
  157.2 0.0 reduce-scatter.2.cloned.1.call-update
  157.3 0.0 all-gather.5.cloned.1.call-start
  157.3 0.9 copy-done.1
  158.2 0.1 copy.11
  158.3 0.0 copy-done.2
  158.3 0.1 copy.12
  158.5 0.0 copy-done.3
  158.5 50.7 %reduce-scatter.2.cloned.1.call-done = f32[512,512]{0,1:T(8,128)} async-done(((f32[4096,512]{0,1:T(8,128)}), f32[512,512]{0,1:T(8,128)}) %reduce-scatter.2.cloned.1.call-update) | async-done | bytes 1048592 | tf_op jit(solution)/shard_map/reduce_scatter | solution.py:19
  209.3 0.0 copy-start
  209.3 1.2 multiply_reduce_fusion.4
  210.5 61.0 %psum.42 = f32[512]{0:T(512)S(1)} all-reduce(f32[512]{0:T(512)S(1)} %multiply_reduce_fusion.4), channel_id=1, replica_groups=mesh['fsdp'=32,'tp'=8] {'fsdp'}, use_global_device_ids=true, to_apply=%region_2.0 | all-reduce | flops 512 | bytes 4096 | tf_op jit(solution)/shard_map/psum | solution.py:30
  271.5 1.3 multiply_reduce_fusion.3
  272.8 55.7 %psum.43 = f32[512]{0:T(512)S(1)} all-reduce(f32[512]{0:T(512)S(1)} %multiply_reduce_fusion.3), channel_id=1, replica_groups=mesh['fsdp'=32,'tp'=8] {'fsdp'}, use_global_device_ids=true, to_apply=%region_4.0 | all-reduce | flops 512 | bytes 4096 | tf_op jit(solution)/shard_map/psum | solution.py:34
  328.5 0.0 copy-done
  328.5 0.3 multiply_reduce_fusion.2
  328.9 57.9 %all-reduce = (f32[512]{0:T(512)S(1)}, f32[512]{0:T(512)S(1)}) all-reduce(f32[512]{0:T(512)S(1)} %get-tuple-element.7, f32[512]{0:T(512)S(1)} %get-tuple-element.6), channel_id=1, replica_groups=mesh['fsdp'=32,'tp'=8] {'fsdp'}, use_global_device_ids=true, to_apply=%region_8.0 | all-reduce | flops 1024 | bytes 8192 | tf_op jit(solution)/shard_map/psum | solution.py:41
  386.8 1.1 divide_convert_fusion
  388.0 0.0 all-gather.5.cloned.1.call-update
  388.0 1.8 copy.14
  389.8 2.7 copy.13
  393.2 56.9 %all-gather.5.cloned.1.call-done = bf16[4096,256]{0,1:T(8,128)(2,1)} async-done(((bf16[512,256]{0,1:T(8,128)(2,1)}), bf16[4096,256]{0,1:T(8,128)(2,1)}) %all-gather.5.cloned.1.call-update) | async-done | bytes 2097168 | tf_op jit(solution)/shard_map/all_gather | solution.py:53
  450.1 12.0 %multiply_reduce_fusion.1 = (f32[]{:T(128)}, f32[1792,256]{0,1:T(8,128)}) fusion(f32[1792,256]{0,1:T(8,128)S(1)} %copy.14, f32[1792,256]{0,1:T(8,128)} %copy.13, f32[]{:T(128)S(6)} %copy.17, bf16[4096,256]{0,1:T(8,128)(2,1)} %all-gather.5.cloned.1.call-done, bf16[4096,1792]{1,0:T(8,128)(2,1)} %all-gather.3.cloned.1.call-done), kind=kOutput, calls=%fused_computation.8 | convolution fusion | flops 3759931392 | bytes 22282248 | tf_op jit(solution)/shard_map/dot_general | solution.py:51
  462.1 76.7 %psum.46 = f32[]{:T(128)} all-reduce(f32[]{:T(128)} %get-tuple-element.13), channel_id=1, replica_groups=mesh['fsdp'=32,'tp'=8] {'fsdp','tp'}, use_global_device_ids=true, to_apply=%region_10.0 | all-reduce | flops 1 | bytes 8 | tf_op jit(solution)/shard_map/psum | solution.py:59
  539.4 2.6 multiply_reduce_fusion
  542.0 73.6 %psum.47 = f32[]{:T(128)} all-reduce(f32[]{:T(128)} %multiply_reduce_fusion), channel_id=1, replica_groups=mesh['fsdp'=32,'tp'=8] {'fsdp','tp'}, use_global_device_ids=true, to_apply=%region_12.0 | all-reduce | flops 1 | bytes 8 | tf_op jit(solution)/shard_map/psum | solution.py:61
  616.3 3.0 broadcast_divide_fusion
  619.2 2.7 copy.16
  (4 shorter events, 0.0 us)
Async XLA Ops:
  7.2 136.9 %copy-start.4 = (bf16[1792,256]{1,0:T(8,128)(2,1)S(1)}, bf16[1792,256]{1,0:T(8,128)(2,1)}, u32[]{:S(2)}) copy-start(bf16[1792,256]{1,0:T(8,128)(2,1)} %param.12) | copy-start | bytes 2752516
  7.2 136.9 %all-gather.3.cloned.1.call-start = ((), (), s32[]{:S(2)}) async-start(), calls=%async_computation.1 | async-start | bytes 15138816 | tf_op jit(solution)/shard_map/all_gather | solution.py:16
  7.9 201.3 %reduce-scatter.2.cloned.1.call-start = ((), (), s32[]{:S(2)}) async-start(), calls=%async_computation.2 | async-start | bytes 9437184 | tf_op jit(solution)/shard_map/reduce_scatter | solution.py:19
  157.2 0.9 copy-start.1
  157.2 1.1 copy-start.2
  157.2 1.3 copy-start.3
  157.3 292.8 %all-gather.5.cloned.1.call-start = ((), (), s32[]{:S(2)}) async-start(), calls=%async_computation.3 | async-start | bytes 2359296 | tf_op jit(solution)/shard_map/all_gather | solution.py:53
  209.3 119.3 %copy-start = (f32[512,512]{0,1:T(8,128)S(1)}, f32[512,512]{0,1:T(8,128)}, u32[]{:S(2)}) copy-start(f32[512,512]{0,1:T(8,128)} %reduce-scatter.2.cloned.1.call-done) | copy-start | bytes 3145732
Sparse Core Ops, SparseCore 0:
  10.6 133.4 all-gather.2
  157.4 51.8 reduce-scatter.1
  388.1 61.9 all-gather.4
where the time goes:
time: 631 us
  blocking collectives  325 us (52%)
  waiting for transfers between devices  243 us (39%)
  matrix products  25.2 us (4%)
  between operations  18.1 us (3%)
  other arithmetic  11.2 us (2%)
  local copies, waits for them, and re-layouts  8.43 us (1%)
    all_gather x1, waiting for transfers between devices, on_device(): gathered = lax.all_gather(hidden, 'fsdp', axis=0, tiled=True)  135 us
    psum x1, blocking collectives, on_device(): alpha = lax.psum(jnp.sum(update * v_cur), ('fsdp', 'tp')) * scale  76.7 us
    psum x1, blocking collectives, on_device(): beta = jnp.sqrt(lax.psum(jnp.sum(update * update), ('fsdp', 'tp')) * scale)  73.6 us
    psum x1, blocking collectives, on_device(): squares = lax.psum(jnp.sum(outputs * outputs, axis=1), 'fsdp')  61 us
    psum x1, blocking collectives, on_device(): lax.psum(jnp.sum(normed_dot * adjoint + normed * adjoint_dot, axis=1), 'f...  57.9 us
    all_gather x1, waiting for transfers between devices, on_device(): lax.all_gather(hessian_rows, 'tp', axis=0, tiled=True)  56.9 us
    psum x1, blocking collectives, on_device(): lax.psum((jnp.sum(normed * adjoint, axis=1), jnp.sum(normed * tangent, ax...  55.7 us
    reduce_scatter x1, waiting for transfers between devices, on_device(): lax.psum_scatter(jnp.dot(block_rows, stacked, preferred_element_type=jnp....  50.7 us
  transfers between devices with their start and end apart: 3, of which 3 were waited for; matrix products, arithmetic and copies ran while one was open for 1% of the time, Pallas kernels for 0%

commit v1 on v0

v1 whole, which is shorter than its diff:
```python
import jax
import jax.numpy as jnp
from jax import lax
from jax.sharding import PartitionSpec as P

D = 8192
FF = 14336


EPSILON = 1e-05


def on_device(hidden, residual, target, norm_gain, weight, v_prev, v_cur, beta_prev):
    columns = weight.shape[1]
    stacked = jnp.concatenate([weight, v_cur.astype(jnp.bfloat16)], axis=1)
    gathered = lax.all_gather(hidden, "fsdp", axis=0, tiled=True)
    total_rows = gathered.shape[0]
    sums = lax.psum_scatter(
        jnp.dot(gathered, stacked, preferred_element_type=jnp.float32),
        "tp",
        scatter_dimension=0,
        tiled=True,
    )
    o = residual.astype(jnp.float32) + sums[:, :columns]
    t = sums[:, columns:]
    y = target.astype(jnp.float32) * norm_gain
    g2 = norm_gain * norm_gain
    parts = jnp.stack(
        [
            jnp.sum(o * o, axis=1),
            jnp.sum(g2 * o * o, axis=1),
            jnp.sum(y * o, axis=1),
            jnp.sum(o * t, axis=1),
            jnp.sum(g2 * o * t, axis=1),
            jnp.sum(y * t, axis=1),
        ]
    )
    s_oo, s_goo, s_yo, s_ot, s_got, s_yt = lax.psum(parts, "fsdp")[:, :, None]
    inv = 1.0 / jnp.sqrt(s_oo / D + EPSILON)
    stretch = s_ot * inv / D
    centre = (s_goo * inv - s_yo) * inv / D
    tilt = stretch * inv
    centre_dot = (2.0 * inv * s_got - s_yt + tilt * (s_yo - 2.0 * inv * s_goo)) * inv / D
    normed = o * inv
    normed_dot = (t - normed * stretch) * inv
    rows = (
        (g2 - centre) * (normed_dot - normed * tilt) - normed * centre_dot + y * tilt
    ) * (inv / total_rows)
    rows = rows.astype(jnp.bfloat16)
    product = lax.dot_general(
        gathered,
        lax.all_gather(rows, "tp", axis=0, tiled=True),
        (((0,), (0,)), ((), ())),
        preferred_element_type=jnp.float32,
    )
    scale = 1.0 / (FF * D)
    update = product - beta_prev * v_prev
    v_sq = jnp.sum(v_cur * v_cur)
    along = jnp.sum(update * v_cur)
    own = along / jnp.maximum(v_sq, 1e-30)
    left = update - own * v_cur
    facts = jnp.stack([v_sq, along, own, jnp.sum(left * left), jnp.sum(left * v_cur)])
    facts = lax.all_gather(facts, ("fsdp", "tp"))
    alpha = jnp.sum(facts[:, 1]) * scale
    shift = facts[:, 2] - alpha
    beta = jnp.sqrt(
        jnp.sum(facts[:, 3] + shift * (shift * facts[:, 0] + 2.0 * facts[:, 4])) * scale
    )
    return ((update - alpha * v_cur) / beta, alpha, beta)


def solution(mesh):
    return jax.shard_map(
        on_device,
        mesh=mesh,
        in_specs=(
            P("fsdp", "tp"),
            P("tp", "fsdp"),
            P("tp", "fsdp"),
            P("fsdp"),
            P("tp", "fsdp"),
            P("tp", "fsdp"),
            P("tp", "fsdp"),
            P(),
        ),
        out_specs=(P("tp", "fsdp"), P(), P()),
        check_vma=False,
    )
```

time: 631 us -> 488 us (0.77)
  blocking collectives: 325 us -> 192 us
  waiting for transfers between devices: 243 us -> 227 us
    psum x5 -> x1, blocking collectives: 325 us -> 115 us  [on_device(): s_oo, s_goo, s_yo, s_ot, s_got, s_yt = lax.psum(parts, 'fsdp')[:, :, None]]
    unnamed x0 -> x1, blocking collectives: none -> 76.7 us
    all_gather x1, waiting for transfers between devices: 56.9 us -> 42.3 us  [on_device(): lax.all_gather(rows, 'tp', axis=0, tiled=True)]
  transfers between devices with their start and end apart: 3 -> 3, of which waited for: 3 -> 3; matrix products, arithmetic and copies ran while one was open for 1% -> 2% of each run, Pallas kernels for 0% -> 0%
where the time goes in v1:
time: 488 us
  waiting for transfers between devices  227 us (47%)
  blocking collectives  192 us (39%)
  matrix products  25.2 us (5%)
  between operations  19.4 us (4%)
  other arithmetic  13 us (3%)
  local copies, waits for them, and re-layouts  11.4 us (2%)
    all_gather x1, waiting for transfers between devices, on_device(): gathered = lax.all_gather(hidden, 'fsdp', axis=0, tiled=True)  133 us
    psum x1, blocking collectives, on_device(): s_oo, s_goo, s_yo, s_ot, s_got, s_yt = lax.psum(parts, 'fsdp')[:, :, None]  115 us
    unnamed x1, blocking collectives  76.7 us
    reduce_scatter x1, waiting for transfers between devices, on_device(): lax.psum_scatter(jnp.dot(gathered, stacked, preferred_element_type=jnp.fl...  50.8 us
    all_gather x1, waiting for transfers between devices, on_device(): lax.all_gather(rows, 'tp', axis=0, tiled=True)  42.3 us
    dot_general x1, matrix products, on_device(): jnp.dot(gathered, stacked, preferred_element_type=jnp.float32)  13.1 us
    dot_general x1, matrix products, on_device(): lax.dot_general(gathered, lax.all_gather(rows, 'tp', axis=0, tiled=True),...  12 us
  transfers between devices with their start and end apart: 3, of which 3 were waited for; matrix products, arithmetic and copies ran while one was open for 2% of the time, Pallas kernels for 0%

profile of v1, /device:TPU:1, one launch (start us, length us, event | category | flops | bytes accessed | tf_op | source)
XLA Modules:
  0.0 488.0 jit_solution(13138185865936434768)
XLA Ops:
  7.2 0.0 copy-start.4
  7.2 0.0 all-gather.4.cloned.1.call-start
  7.2 0.7 all-gather.4.cloned.1.call-update
  7.9 0.0 reduce-scatter.2.cloned.1.call-start
  8.0 3.1 multiply_reduce_fusion.3
  11.1 133.0 %all-gather.4.cloned.1.call-done = bf16[4096,1792]{1,0:T(8,128)(2,1)} async-done(((bf16[128,1792]{1,0:T(8,128)(2,1)}), bf16[4096,1792]{1,0:T(8,128)(2,1)}) %all-gather.4.cloned.1.call-update) | async-done | bytes 14680080 | tf_op jit(solution)/shard_map/all_gather | solution.py:16
  144.1 0.0 copy-done.4
  144.1 13.1 %convolution_bitcast_fusion = f32[4096,512]{0,1:T(8,128)} fusion(bf16[4096,1792]{1,0:T(8,128)(2,1)} %all-gather.4.cloned.1.call-done, bf16[1792,256]{1,0:T(8,128)(2,1)S(1)} %get-tuple-element.23, bf16[1792,256]{1,0:T(8,128)(2,1)S(1)} %copy-done.4), kind=kOutput, calls=%fused_computation | convolution fusion | flops 7519862784 | bytes 24903680 | tf_op jit(solution)/shard_map/dot_general | solution.py:19
  157.2 0.0 copy-start.1
  157.2 0.0 copy-start.3
  157.2 0.0 copy-start.2
  157.2 0.0 reduce-scatter.2.cloned.1.call-update
  157.3 0.0 all-gather.6.cloned.1.call-start
  157.3 0.9 copy-done.1
  158.2 0.1 copy.20
  158.3 0.0 copy-done.3
  158.3 0.0 copy-done.2
  158.4 0.1 copy.19
  158.5 50.8 %reduce-scatter.2.cloned.1.call-done = f32[512,512]{0,1:T(8,128)} async-done(((f32[4096,512]{0,1:T(8,128)}), f32[512,512]{0,1:T(8,128)}) %reduce-scatter.2.cloned.1.call-update) | async-done | bytes 1048592 | tf_op jit(solution)/shard_map/reduce_scatter | solution.py:18
  209.3 0.0 copy-start
  209.3 1.6 fusion.5
  210.9 115.4 %psum.7 = f32[6,512]{1,0:T(8,128)S(1)} all-reduce(f32[6,512]{1,0:T(8,128)S(1)} %stack.45), channel_id=1, replica_groups=mesh['fsdp'=32,'tp'=8] {'fsdp'}, use_global_device_ids=true, to_apply=%region_7.0 | all-reduce | flops 3072 | bytes 24576 | tf_op jit(solution)/shard_map/psum | solution.py:38
  326.4 0.0 copy-done
  326.4 1.0 multiply_convert_fusion
  327.4 0.0 all-gather.6.cloned.1.call-update
  327.4 1.8 copy.22
  329.2 2.7 copy.21
  333.3 42.3 %all-gather.6.cloned.1.call-done = bf16[4096,256]{0,1:T(8,128)(2,1)} async-done(((bf16[512,256]{0,1:T(8,128)(2,1)}), bf16[4096,256]{0,1:T(8,128)(2,1)}) %all-gather.6.cloned.1.call-update) | async-done | bytes 2097168 | tf_op jit(solution)/shard_map/all_gather | solution.py:52
  375.5 12.0 %multiply_reduce_fusion.2 = (f32[]{:T(128)}, f32[1792,256]{0,1:T(8,128)}) fusion(f32[1792,256]{0,1:T(8,128)S(1)} %copy.22, f32[1792,256]{0,1:T(8,128)} %copy.21, f32[]{:T(128)S(6)} %copy.28, bf16[4096,256]{0,1:T(8,128)(2,1)} %all-gather.6.cloned.1.call-done, bf16[4096,1792]{1,0:T(8,128)(2,1)} %all-gather.4.cloned.1.call-done), kind=kOutput, calls=%fused_computation.10 | convolution fusion | flops 3759931392 | bytes 22282248 | tf_op jit(solution)/shard_map/dot_general | solution.py:50
  388.2 2.6 multiply_reduce_fusion
  390.8 2.6 stack.51
  393.4 0.2 dynamic-update-slice
  393.6 76.7 %all-reduce = f32[1280]{0:T(1024)S(1)} all-reduce(f32[1280]{0:T(1024)S(1)} %dynamic-update-slice), channel_id=2, replica_groups=mesh['fsdp'=32,'tp'=8] {'fsdp','tp'}, use_global_device_ids=true, to_apply=%add | all-reduce | flops 1280 | bytes 10240
  470.3 0.2 reshape.130
  470.5 0.7 slice_reduce_fusion.2
  471.9 0.3 slice_reduce_fusion
  472.2 0.6 add_reduce_fusion
  473.5 3.0 subtract_divide_fusion
  476.5 2.7 copy.26
  (5 shorter events, 0.1 us)
Async XLA Ops:
  7.2 136.9 %copy-start.4 = (bf16[1792,256]{1,0:T(8,128)(2,1)S(1)}, bf16[1792,256]{1,0:T(8,128)(2,1)}, u32[]{:S(2)}) copy-start(bf16[1792,256]{1,0:T(8,128)(2,1)} %param.12) | copy-start | bytes 2752516
  7.2 136.9 %all-gather.4.cloned.1.call-start = ((), (), s32[]{:S(2)}) async-start(), calls=%async_computation.1 | async-start | bytes 15138816 | tf_op jit(solution)/shard_map/all_gather | solution.py:16
  7.9 201.4 %reduce-scatter.2.cloned.1.call-start = ((), (), s32[]{:S(2)}) async-start(), calls=%async_computation.2 | async-start | bytes 9437184 | tf_op jit(solution)/shard_map/reduce_scatter | solution.py:18
  157.2 0.9 copy-start.1
  157.2 1.1 copy-start.3
  157.2 1.1 copy-start.2
  157.3 218.3 %all-gather.6.cloned.1.call-start = ((), (), s32[]{:S(2)}) async-start(), calls=%async_computation.3 | async-start | bytes 2359296 | tf_op jit(solution)/shard_map/all_gather | solution.py:52
  209.3 117.1 %copy-start = (f32[512,512]{0,1:T(8,128)S(1)}, f32[512,512]{0,1:T(8,128)}, u32[]{:S(2)}) copy-start(f32[512,512]{0,1:T(8,128)} %reduce-scatter.2.cloned.1.call-done) | copy-start | bytes 3145732
Sparse Core Ops, SparseCore 0:
  10.6 133.4 all-gather.3
  157.4 51.8 reduce-scatter.1
  327.5 47.9 all-gather.5

commit v2 on v0

v2 whole, which is shorter than its diff:
```python
import functools

import jax
import jax.numpy as jnp
from jax import lax
from jax.experimental import pallas as pl
from jax.experimental.pallas import tpu as pltpu
from jax.sharding import PartitionSpec as P

D = 8192
FF = 14336
EPSILON = 1e-05

NY, NZ, NT = 4, 8, 8
STAGES = 4
SPLIT = 1024
LEAD = 1
SCHEDULE = [
    (0, -1), (1, 0), ("pair", 6), (2, 1), ("stats", 6), (3, 2), ("stats_y", 6), (4, 3),
    ("hessian", 6), (5, 4), ("share", 6), (6, 5), ("forward", 5), ("backward", 6),
]
BF, F32 = jnp.bfloat16, jnp.float32
MESH = pl.DeviceIdType.MESH


def gather_plan(ff):
    cols = {"a": (0, SPLIT), "b": (SPLIT, ff - SPLIT)}
    size = {"y": NY, "z": NZ}
    order = {"a": ("z", "y"), "b": ("y", "z")}
    slots = {}

    def slot(key):
        return slots.setdefault(key, len(slots))

    def arrivals(part, first, second):
        axes = order[part]
        start, width = cols[part]
        offs = (first, second)
        level = 1 if second else 0
        off, n = offs[level], size[axes[level]]
        if abs(off) * 2 == n:
            half = width // 2
            return [
                ((part, first, second, 0), (start, half), axes[level], -1),
                ((part, first, second, 1), (start + half, half), axes[level], 1),
            ]
        step = -1 if off > 0 else 1
        return [((part, first, second, 0), (start, width), axes[level], step)]

    def offsets(n):
        return [0] + [s * d for d in range(1, n // 2) for s in (1, -1)] + [n // 2]

    waves = [[] for _ in range(NY // 2 + NZ // 2 + 1)]
    for part in ("b", "a"):
        n1, n2 = (size[axis] for axis in order[part])
        for first in offsets(n1):
            for second in offsets(n2):
                recvs = []
                if first or second:
                    recvs = [(slot(key), c) for key, c, _, _ in arrivals(part, first, second)]
                sends = []

                def forward(nf, ns, step):
                    for key, c, axis, s in arrivals(part, nf, ns):
                        if s == step:
                            sends.append((slot(key), c, axis, step))

                for off, n, grow in (
                    (second, n2, lambda o: (first, o)),
                    (first, n1, lambda o: (o, 0)),
                ):
                    if grow(0)[1] == 0 and grow(1)[1] == 0 and second:
                        continue
                    if off >= 0 and off < n // 2:
                        forward(*grow(off + 1), -1)
                    if off <= 0 and -off < n // 2:
                        o = off - 1
                        forward(*grow(n // 2 if -o == n // 2 else o), 1)
                where = (first, second) if order[part][0] == "y" else (second, first)
                waves[abs(first) + abs(second)].append((where, recvs, sends))
    return waves, len(slots)

def kernel(
    hidden, residual, target, gain, weight, v_prev, v_cur, beta_prev,
    update, facts_out,
    hid, w, vb, vc, vp, res, tar, sib_out, sib_in, half, x_out, x_in, o_s, t_s, stat_z, stat_y,
    rows_s, prod, fact_z, fact_y, fact_t,
    local_sem, hid_recv, sib_recv, x_recv, z_recv, y_recv, rows_recv, fact_recv,
    send_sem, fact_send,
):
    stages, n_blocks, rows, ff = hid.shape
    four = 4 * rows
    cols = w.shape[1]
    tokens = stages * n_blocks * rows
    fs, tp = lax.axis_index("fsdp"), lax.axis_index("tp")
    y, z = fs // NZ, fs % NZ
    x, core = tp // 2, tp % 2
    waves, _ = gather_plan(ff)
    ys = [(y + d) % NY for d in range(NY)]
    zs = [(z + d) % NZ for d in range(NZ)]
    z_place = [(q // 4) * 16 + q % 4 for q in zs]

    def place(dy, dz):
        return z_place[dz % NZ] + ys[dy % NY] * 4

    me = place(0, 0)

    def at(dy=0, dz=0):
        return (ys[dy % NY] * NZ + zs[dz % NZ], tp)

    def at_x(dx):
        return (fs, ((x + dx) % 4) * 2 + core)

    sibling = (fs, x * 2 + 1 - core)

    loads = [
        pltpu.make_async_copy(hidden.at[pl.ds(k * rows, rows)], hid.at[k, me], local_sem.at[k])
        for k in range(stages)
    ]
    for n, (src, dst) in enumerate(
        ((weight, w), (v_cur, vc), (residual, res), (target, tar), (v_prev, vp))
    ):
        loads.append(pltpu.make_async_copy(src, dst, local_sem.at[stages + n]))
    for load in loads:
        load.start()

    barrier = pltpu.get_barrier_semaphore()
    peers = [at(dy=d) for d in range(1, NY)] + [at(dz=d) for d in range(1, NZ)]
    peers += [(fs, (tp + d) % NT) for d in range(1, NT)]
    for peer in peers:
        pl.semaphore_signal(barrier, inc=1, device_id=peer, device_id_type=MESH)
    pl.semaphore_wait(barrier, len(peers))

    def remote(src, dst, send, recv, to):
        return pltpu.make_async_remote_copy(
            src_ref=src, dst_ref=dst, send_sem=send, recv_sem=recv,
            device_id=to, device_id_type=MESH,
        )

    def hid_copy(k, block, slot, columns, to):
        ref = hid.at[k, block, :, pl.ds(*columns)]
        return remote(ref, ref, send_sem.at[0, k], hid_recv.at[k, slot], to)

    def wave(d, k):
        for where, recvs, sends in waves[d]:
            block = place(*where)
            for slot, columns in recvs:
                hid_copy(k, block, slot, columns, sibling).wait_recv()
            for slot, columns, axis, step in sends:
                to = at(dy=step) if axis == "y" else at(dz=step)
                hid_copy(k, block, slot, columns, to).start()

    def dot_rows(k, c, write):
        def tile(i, carry):
            lhs = hid[k, pl.ds(c * 16 + i * 8, 8)].reshape(8 * rows, ff)
            for n, rhs in enumerate((w, vb)):
                out = jnp.dot(lhs, rhs[...], preferred_element_type=F32)
                write(i, n, out.reshape(2, four, cols))
            return carry

        lax.fori_loop(0, 2, tile, 0)

    def sib_copy(k):
        return remote(sib_out.at[k], sib_in.at[k], send_sem.at[1, k], sib_recv.at[k], sibling)

    def forward(k):
        def to_sibling(i, n, out):
            sib_out[k, pl.ds(i * 2, 2), :, pl.ds(n * cols, cols)] = out.astype(BF)

        def to_half(i, n, out):
            half[pl.ds(i * 2, 2), :, pl.ds(n * cols, cols)] = out

        dot_rows(k, 1 - core, to_sibling)
        sib_copy(k).start()
        dot_rows(k, core, to_half)

    def x_copy(k, dx, slot):
        there = (x + dx) % 4
        return remote(
            x_out.at[k, there], x_in.at[k, slot], send_sem.at[2, k], x_recv.at[k, slot], at_x(dx)
        )

    def pair(k):
        sib_copy(k).wait_recv()
        for dx in (2, 1, 3):
            there = (x + dx) % 4
            x_out[k, there] = (half[there] + sib_in[k, there].astype(F32)).astype(BF)
            x_copy(k, dx, x).start()
        half[x] = half[x] + sib_in[k, x].astype(F32)

    def token_rows(ref, k):
        return jnp.concatenate(
            [ref[pl.ds(j * stages * rows + k * rows, rows), :].astype(F32) for j in range(4)], axis=0
        )

    def z_copy(k, dz):
        src = stat_z.at[k, z]
        return remote(src, src, send_sem.at[3, k], z_recv.at[k, z], at(dz=dz))

    def y_copy(k, dy):
        src = stat_y.at[k, y]
        return remote(src, src, send_sem.at[4, k], y_recv.at[k, y], at(dy=dy))

    lane = lax.broadcasted_iota(jnp.int32, (four, 128), 1)

    def stats(k):
        total = half[x]
        for dx in (1, 3, 2):
            there = (x + dx) % 4
            x_copy(k, dx, there).wait_recv()
            total = total + x_in[k, there].astype(F32)
        o = total[:, :cols] + token_rows(res, k)
        t = total[:, cols:]
        g = gain[...]
        gy = token_rows(tar, k) * g
        o_s[k] = o
        t_s[k] = t
        g2o = g * g * o
        packed = jnp.zeros((four, 128), F32)
        for n, term in enumerate((o * o, g2o * o, gy * o, o * t, g2o * t, gy * t)):
            packed = jnp.where(lane == n, jnp.sum(term, axis=1, keepdims=True), packed)
        stat_z[k, z] = packed.T[:8]
        for dz in (4, 3, 5, 2, 6, 1, 7):
            z_copy(k, dz).start()

    def stats_y(k):
        for dz in range(1, NZ):
            there = zs[dz]
            ref = stat_z.at[k, there]
            remote(ref, ref, send_sem.at[3, k], z_recv.at[k, there], sibling).wait_recv()
        stat_y[k, y] = jnp.sum(stat_z[k], axis=0)
        for dy in (2, 1, 3):
            y_copy(k, dy).start()

    def rows_copy(k, cc, xx, sem, to):
        ref = rows_s.at[k, cc * 4 + xx]
        return remote(ref, ref, send_sem.at[5, k], rows_recv.at[k, sem], to)

    def hessian(k):
        for dy in range(1, NY):
            there = ys[dy]
            ref = stat_y.at[k, there]
            remote(ref, ref, send_sem.at[4, k], y_recv.at[k, there], sibling).wait_recv()
        sums = jnp.sum(stat_y[k], axis=0)
        s_oo, s_goo, s_yo, s_ot, s_got, s_yt = (sums[n : n + 1] for n in range(6))
        inv = 1.0 / jnp.sqrt(s_oo / D + EPSILON)
        stretch = s_ot * inv / D
        centre = (s_goo * inv - s_yo) * inv / D
        tilt = stretch * inv
        centre_dot = (2.0 * inv * s_got - s_yt + tilt * (s_yo - 2.0 * inv * s_goo)) * inv / D
        k1 = inv * inv / tokens
        coef = jnp.concatenate(
            [centre, k1, -2.0 * tilt * k1, -centre_dot * k1, tilt * inv / tokens]
            + [jnp.zeros((123, four), F32)],
            axis=0,
        ).T
        o, t, g = o_s[k], t_s[k], gain[...]
        gy = token_rows(tar, k) * g
        out = (g * g - coef[:, 0:1]) * (t * coef[:, 1:2] + o * coef[:, 2:3])
        out = out + o * coef[:, 3:4] + gy * coef[:, 4:5]
        rows_s[k, core * 4 + x] = out.astype(BF)
        for dx in (2, 1, 3):
            rows_copy(k, core, x, x, at_x(dx)).start()
        rows_copy(k, core, x, 4 + x, sibling).start()

    def share(k):
        for dx in (1, 3, 2):
            there = (x + dx) % 4
            rows_copy(k, core, there, there, sibling).wait_recv()
            rows_copy(k, core, there, 4 + there, sibling).start()

    def backward(k):
        for xx in range(4):
            rows_copy(k, 1 - core, xx, 4 + xx, sibling).wait_recv()
        rhs = rows_s[k].reshape(n_blocks * rows, cols)

        def tile(i, carry):
            at_cols = pl.ds(pl.multiple_of(i * 256, 256), 256)
            lhs = hid[k, :, :, at_cols].reshape(n_blocks * rows, 256)
            prod[at_cols, :] += lax.dot_general(
                lhs, rhs, (((0,), (0,)), ((), ())), preferred_element_type=F32
            )
            return carry

        lax.fori_loop(0, ff // 256, tile, 0)

    ops = dict(forward=forward, pair=pair, stats=stats, stats_y=stats_y, hessian=hessian,
               share=share, backward=backward)

    for k in range(stages):
        loads[k].wait()
    for k in range(min(LEAD, stages)):
        wave(0, k)
    for load in loads[stages:]:
        load.wait()
    vb[...] = vc[...].astype(BF)
    prod[...] = -beta_prev[0] * vp[...]

    def body(i, carry):
        for op, lag in SCHEDULE:
            @pl.when((i >= lag) & (i < stages + lag))
            def _(op=op, lag=lag):
                if isinstance(op, int):
                    wave(op, i - lag)
                else:
                    ops[op](i - lag)

        return carry

    lax.fori_loop(0, stages + max(lag for _, lag in SCHEDULE), body, 0)

    out_copy = pltpu.make_async_copy(prod, update, local_sem.at[stages + 5])
    out_copy.start()
    u, v = prod[...], vc[...]
    v_sq = jnp.sum(v * v)
    along = jnp.sum(u * v)
    own = along / jnp.maximum(v_sq, 1e-30)
    left = u - own * v
    lanes = lax.broadcasted_iota(jnp.int32, (8, 128), 1)
    packed = jnp.zeros((8, 128), F32)
    for n, fact in enumerate((v_sq, along, own, jnp.sum(left * left), jnp.sum(left * v))):
        packed = jnp.where(lanes == n, fact, packed)

    def fact_copy(level, ref, n, to):
        return remote(ref, ref, fact_send.at[level], fact_recv.at[level, n], to)

    fact_z[z] = packed
    for dz in (4, 3, 5, 2, 6, 1, 7):
        fact_copy(0, fact_z.at[z], z, at(dz=dz)).start()
    for dz in range(1, NZ):
        fact_copy(0, fact_z.at[zs[dz]], zs[dz], sibling).wait_recv()
    fact_y[y] = jnp.concatenate([fact_z[n, 0:1, :] for n in range(NZ)], axis=0)
    for dy in (2, 1, 3):
        fact_copy(1, fact_y.at[y], y, at(dy=dy)).start()
    for dy in range(1, NY):
        fact_copy(1, fact_y.at[ys[dy]], ys[dy], sibling).wait_recv()
    fact_t[tp] = fact_y[...].reshape(NY * NZ, 128)
    for d in (4, 5, 3, 2, 6, 7, 1):
        fact_copy(2, fact_t.at[tp], tp, (fs, (tp + d) % NT)).start()
    for d in range(1, NT):
        there = (tp + d) % NT
        fact_copy(2, fact_t.at[there], there, sibling).wait_recv()
    facts = fact_t[...].reshape(NT * NY * NZ, 128)
    scale = 1.0 / (FF * D)
    alpha = jnp.sum(facts[:, 1:2], axis=0, keepdims=True) * scale
    shift = facts[:, 2:3] - alpha
    square = facts[:, 3:4] + shift * (shift * facts[:, 0:1] + 2.0 * facts[:, 4:5])
    beta = jnp.sqrt(jnp.sum(square, axis=0, keepdims=True) * scale)
    facts_out[...] = jnp.where(lanes == 0, alpha, beta)

    def sent(ref, sem):
        pltpu.make_async_copy(ref, ref, sem).wait()

    out_copy.wait()
    for k in range(stages):
        sent(hid.at[k, pl.ds(0, n_blocks - 1)], send_sem.at[0, k])
        sent(sib_out.at[k], send_sem.at[1, k])
        sent(x_out.at[k, pl.ds(0, 3)], send_sem.at[2, k])
        sent(stat_z.at[k, pl.ds(0, 7)], send_sem.at[3, k])
        sent(stat_y.at[k, pl.ds(0, 3)], send_sem.at[4, k])
        sent(rows_s.at[k, pl.ds(0, 7)], send_sem.at[5, k])
    sent(fact_z.at[pl.ds(0, 7)], fact_send.at[0])
    sent(fact_y.at[pl.ds(0, 3)], fact_send.at[1])
    sent(fact_t.at[pl.ds(0, 7)], fact_send.at[2])


def on_device(hidden, residual, target, norm_gain, weight, v_prev, v_cur, beta_prev):
    tokens, ff = hidden.shape
    cols = weight.shape[1]
    rows, blocks = tokens // STAGES, NY * NZ
    _, slots = gather_plan(ff)
    dma = pltpu.SemaphoreType.DMA
    anywhere, vmem = pl.BlockSpec(memory_space=pl.ANY), pl.BlockSpec(memory_space=pltpu.VMEM)
    update, facts = pl.pallas_call(
        kernel,
        out_shape=(jax.ShapeDtypeStruct((ff, cols), F32), jax.ShapeDtypeStruct((8, 128), F32)),
        in_specs=[anywhere] * 3 + [vmem] + [anywhere] * 3 + [pl.BlockSpec(memory_space=pltpu.SMEM)],
        out_specs=(anywhere, vmem),
        scratch_shapes=[
            pltpu.VMEM((STAGES, blocks, rows, ff), BF),
            pltpu.VMEM((ff, cols), BF),
            pltpu.VMEM((ff, cols), BF),
            pltpu.VMEM((ff, cols), F32),
            pltpu.VMEM((ff, cols), F32),
            pltpu.VMEM(residual.shape, BF),
            pltpu.VMEM(target.shape, BF),
            pltpu.VMEM((STAGES, 4, 4 * rows, 2 * cols), BF),
            pltpu.VMEM((STAGES, 4, 4 * rows, 2 * cols), BF),
            pltpu.VMEM((4, 4 * rows, 2 * cols), F32),
            pltpu.VMEM((STAGES, 4, 4 * rows, 2 * cols), BF),
            pltpu.VMEM((STAGES, 4, 4 * rows, 2 * cols), BF),
            pltpu.VMEM((STAGES, 4 * rows, cols), F32),
            pltpu.VMEM((STAGES, 4 * rows, cols), F32),
            pltpu.VMEM((STAGES, NZ, 8, 4 * rows), F32),
            pltpu.VMEM((STAGES, NY, 8, 4 * rows), F32),
            pltpu.VMEM((STAGES, 8, 4 * rows, cols), BF),
            pltpu.VMEM((ff, cols), F32),
            pltpu.VMEM((NZ, 8, 128), F32),
            pltpu.VMEM((NY, NZ, 128), F32),
            pltpu.VMEM((NT, NY * NZ, 128), F32),
            dma((STAGES + 6,)),
            dma((STAGES, slots)),
            dma((STAGES,)),
            dma((STAGES, 4)),
            dma((STAGES, NZ)),
            dma((STAGES, NY)),
            dma((STAGES, 8)),
            dma((3, 8)),
            dma((6, STAGES)),
            dma((3,)),
        ],
        compiler_params=pltpu.CompilerParams(
            collective_id=0, has_side_effects=True, vmem_limit_bytes=60 << 20
        ),
    )(
        hidden, residual, target, norm_gain.reshape(1, cols), weight, v_prev, v_cur,
        beta_prev.reshape(1),
    )
    alpha, beta = facts[0, 0], facts[0, 1]
    return (update - alpha * v_cur) / beta, alpha, beta


def solution(mesh):
    return jax.shard_map(
        on_device,
        mesh=mesh,
        in_specs=(
            P("fsdp", "tp"),
            P("tp", "fsdp"),
            P("tp", "fsdp"),
            P("fsdp"),
            P("tp", "fsdp"),
            P("tp", "fsdp"),
            P("tp", "fsdp"),
            P(),
        ),
        out_specs=(P("tp", "fsdp"), P(), P()),
        check_vma=False,
    )
```

time: 631 us -> 209 us (0.33)
  blocking collectives: 325 us -> 0 us
  waiting for transfers between devices: 243 us -> 0 us
  Pallas kernels: 0 us -> 202 us
  matrix products: 25.2 us -> 0 us
  between operations: 18.1 us -> 1.3 us
  local copies, waits for them, and re-layouts: 8.43 us -> 1.33 us
  other arithmetic: 11.2 us -> 4.26 us
    psum x5 -> x0, blocking collectives: 325 us -> none  [the longest x1 76.7 us: on_device(): alpha = lax.psum(jnp.sum(update * v_cur), ('fsdp', 'tp')) * scale]
    pallas_call x0 -> x1, Pallas kernels: none -> 202 us  [on_device(): pl.pallas_call(kernel, out_shape=(jax.ShapeDtypeStruct((ff, cols), F32),...]
    all_gather x2 -> x0, waiting for transfers between devices: 191 us -> none  [the longest x1 135 us: on_device(): gathered = lax.all_gather(hidden, 'fsdp', axis=0, tiled=True)]
    reduce_scatter x1 -> x0, waiting for transfers between devices: 50.7 us -> none  [on_device(): lax.psum_scatter(jnp.dot(block_rows, stacked, preferred_element_type=jnp....]
    dot_general x2 -> x0, matrix products: 25.2 us -> none  [the longest x1 13.1 us: on_device(): jnp.dot(block_rows, stacked, preferred_element_type=jnp.float32)]
    unnamed x15 -> x2, local copies, waits for them, and re-layouts: 8.43 us -> 0.01 us
  transfers between devices with their start and end apart: 3 -> 0, of which waited for: 3 -> 0; matrix products, arithmetic and copies ran while one was open for 1% -> 0% of each run, Pallas kernels for 0% -> 0%
where the time goes in v2:
time: 209 us
  Pallas kernels  202 us (97%)
  other arithmetic  4.26 us (2%)
    pallas_call x1, Pallas kernels, on_device(): pl.pallas_call(kernel, out_shape=(jax.ShapeDtypeStruct((ff, cols), F32),...  202 us
    div x1, other arithmetic, on_device(): return ((update - alpha * v_cur) / beta, alpha, beta)  4.26 us

profile of v2, /device:TPU:1, one launch (start us, length us, event | category | flops | bytes accessed | tf_op | source)
XLA Modules:
  0.0 209.1 jit_solution(17593929413497881558)
XLA Ops:
  1.3 0.0 copy-start
  1.3 202.2 %shard_map.103 = (f32[1792,256]{1,0:T(8,128)}, f32[8,128]{1,0:T(8,128)}) custom-call(bf16[128,1792]{1,0:T(8,128)(2,1)} %hidden.1, bf16[512,256]{1,0:T(8,128)(2,1)} %residual.1, bf16[512,256]{1,0:T(8,128)(2,1)} %target.1, f32[1,256]{1,0:T(1,128)} %bitcast.5, bf16[1792,256]{1,0:T(8,128)(2,1)} %weight.1, f32[1792,256]{1,0:T(8,128)} %v_prev.1, ...), custom_call_target="tpu_custom_call" | custom-call | tf_op jit(solution)/shard_map/pallas_call | solution.py:374
  203.5 1.3 fusion
  204.9 0.0 copy-done
  204.9 4.3 %subtract_divide_fusion = f32[1792,256]{1,0:T(8,128)} fusion(f32[1792,256]{1,0:T(8,128)} %get-tuple-element.5, f32[1792,256]{1,0:T(8,128)S(1)} %copy-done, f32[]{:T(128)} %bitcast.3, f32[]{:T(128)} %bitcast.2), kind=kLoop, calls=%fused_computation | loop fusion | flops 1376256 | bytes 5505032 | tf_op jit(solution)/shard_map/div | solution.py:420
Async XLA Ops:
  1.3 203.6 %copy-start = (f32[1792,256]{1,0:T(8,128)S(1)}, f32[1792,256]{1,0:T(8,128)}, u32[]{:S(2)}) copy-start(f32[1792,256]{1,0:T(8,128)} %v_cur.1) | copy-start | bytes 5505028

commit v3 on v0

v3 whole, which is shorter than its diff:
```python
import functools

import jax
import jax.numpy as jnp
from jax import lax
from jax.experimental import pallas as pl
from jax.experimental.pallas import tpu as pltpu
from jax.sharding import PartitionSpec as P

D = 8192
FF = 14336
EPSILON = 1e-05

NY, NZ, NT = 4, 8, 8
GROUPS = ((0, 32, 3), (96, 16, 2))
SPLIT = 1024
SCHEDULE = [
    ("prepare", 1), ("pair", 3), ("stats", 4), ("stats_y", 5), ("hessian", 6), ("share", 7),
    ("backward", 8), (0, -1), (1, 0), (3, 1), (5, 2), (2, 0), (4, 1), (6, 2), ("forward", 2),
]
REFS = 17
BF, F32 = jnp.bfloat16, jnp.float32
MESH = pl.DeviceIdType.MESH


def gather_plan(ff):
    cols = {"a": (0, SPLIT), "b": (SPLIT, ff - SPLIT)}
    size = {"y": NY, "z": NZ}
    order = {"a": ("z", "y"), "b": ("y", "z")}
    slots = {}

    def slot(key):
        return slots.setdefault(key, len(slots))

    def arrivals(part, first, second):
        axes = order[part]
        start, width = cols[part]
        offs = (first, second)
        level = 1 if second else 0
        off, n = offs[level], size[axes[level]]
        if abs(off) * 2 == n:
            half = width // 2
            return [
                ((part, first, second, 0), (start, half), axes[level], -1),
                ((part, first, second, 1), (start + half, half), axes[level], 1),
            ]
        step = -1 if off > 0 else 1
        return [((part, first, second, 0), (start, width), axes[level], step)]

    def offsets(n):
        return [0] + [s * d for d in range(1, n // 2) for s in (1, -1)] + [n // 2]

    waves = [[] for _ in range(NY // 2 + NZ // 2 + 1)]
    for part in ("b", "a"):
        n1, n2 = (size[axis] for axis in order[part])
        for first in offsets(n1):
            for second in offsets(n2):
                recvs = []
                if first or second:
                    recvs = [(slot(key), c) for key, c, _, _ in arrivals(part, first, second)]
                sends = []

                def forward(nf, ns, step):
                    for key, c, axis, s in arrivals(part, nf, ns):
                        if s == step:
                            sends.append((slot(key), c, axis, step))

                for off, n, grow in (
                    (second, n2, lambda o: (first, o)),
                    (first, n1, lambda o: (o, 0)),
                ):
                    if grow(0)[1] == 0 and grow(1)[1] == 0 and second:
                        continue
                    if off >= 0 and off < n // 2:
                        forward(*grow(off + 1), -1)
                    if off <= 0 and -off < n // 2:
                        o = off - 1
                        forward(*grow(n // 2 if -o == n // 2 else o), 1)
                where = (first, second) if order[part][0] == "y" else (second, first)
                waves[abs(first) + abs(second)].append((where, recvs, sends))
    return waves, len(slots)

def kernel(
    hidden, residual, target, gain, weight, v_prev, v_cur, beta_prev,
    update, facts_out,
    hid, w, vb, vc, vp, res, tar, prod, fact_fs, fact_t, v_sq, local_sem, fact_recv, fact_send,
    *of_groups,
):
    n_blocks, local, ff = hid.shape
    cols = w.shape[1]
    tokens = n_blocks * local
    fs, tp = lax.axis_index("fsdp"), lax.axis_index("tp")
    y, z = fs // NZ, fs % NZ
    x, core = tp // 2, tp % 2
    waves, _ = gather_plan(ff)
    ys = [(y + d) % NY for d in range(NY)]
    zs = [(z + d) % NZ for d in range(NZ)]
    z_place = [(q // 4) * 16 + q % 4 for q in zs]

    def place(dy, dz):
        return z_place[dz % NZ] + ys[dy % NY] * 4

    me = place(0, 0)

    def at(dy=0, dz=0):
        return (ys[dy % NY] * NZ + zs[dz % NZ], tp)

    def at_x(dx):
        return (fs, ((x + dx) % 4) * 2 + core)

    sibling = (fs, x * 2 + 1 - core)

    loads = [
        pltpu.make_async_copy(src, dst, local_sem.at[n])
        for n, (src, dst) in enumerate(
            (
                (hidden, hid.at[me]), (weight, w), (v_cur, vc), (residual, res), (target, tar),
                (v_prev, vp),
            )
        )
    ]
    for load in loads:
        load.start()

    barrier = pltpu.get_barrier_semaphore()
    others = [(dy, dz) for dz in (4, 3, 5, 2, 6, 1, 7, 0) for dy in (2, 1, 3, 0) if dy or dz]
    peers = [at(1, 0), at(-1, 0), at(0, 1), at(0, -1)] + [(fs, (tp + d) % NT) for d in range(1, NT)]
    for peer in peers:
        pl.semaphore_signal(barrier, inc=1, device_id=peer, device_id_type=MESH)
    pl.semaphore_wait(barrier, len(peers))

    def remote(src, dst, send, recv, to):
        return pltpu.make_async_remote_copy(
            src_ref=src, dst_ref=dst, send_sem=send, recv_sem=recv,
            device_id=to, device_id_type=MESH,
        )

    def sent(ref, sem):
        pltpu.make_async_copy(ref, ref, sem).wait()

    def steps_of(
        first, rows,
        sib_out, sib_in, half, x_out, x_in, o_s, t_s, stat_z, stat_y, rows_s,
        hid_recv, sib_recv, x_recv, z_recv, y_recv, rows_recv, send_sem,
    ):
        four = 4 * rows
        some = max(1, 256 // four)

        def row(k):
            return pl.multiple_of(first + k * rows, 16)

        def span(k):
            return pl.ds(row(k), rows)

        def hid_copy(k, block, slot, columns, to):
            ref = hid.at[block, span(k), pl.ds(*columns)]
            return remote(ref, ref, send_sem.at[0, k], hid_recv.at[k, slot], to)

        def wave(d, k):
            for where, recvs, sends in waves[d]:
                block = place(*where)
                for slot, columns in recvs:
                    hid_copy(k, block, slot, columns, sibling).wait_recv()
                for slot, columns, axis, step in sends:
                    to = at(dy=step) if axis == "y" else at(dz=step)
                    hid_copy(k, block, slot, columns, to).start()

        def dot_rows(k, c, write):
            def tile(i, carry):
                lhs = hid[pl.ds(c * 16 + i * 4 * some, 4 * some), span(k), :].reshape(some * four, ff)
                for n, rhs in enumerate((w, vb)):
                    out = jnp.dot(lhs, rhs[...], preferred_element_type=F32)
                    write(i, n, out.reshape(some, four, cols))
                return carry

            lax.fori_loop(0, 4 // some, tile, 0)

        def sib_copy(k):
            return remote(sib_out.at[k], sib_in.at[k], send_sem.at[1, k], sib_recv.at[k], sibling)

        def forward(k):
            def to_sibling(i, n, out):
                sib_out[k, pl.ds(i * some, some), :, pl.ds(n * cols, cols)] = out.astype(BF)

            def to_half(i, n, out):
                half[k, pl.ds(i * some, some), :, pl.ds(n * cols, cols)] = out

            dot_rows(k, 1 - core, to_sibling)
            sib_copy(k).start()
            dot_rows(k, core, to_half)

        def x_copy(k, dx, slot):
            there = (x + dx) % 4
            return remote(
                x_out.at[k, there], x_in.at[k, slot], send_sem.at[2, k], x_recv.at[k, slot], at_x(dx)
            )

        def pair(k):
            sib_copy(k).wait_recv()
            for dx in (2, 1, 3):
                there = (x + dx) % 4
                x_out[k, there] = (half[k, there] + sib_in[k, there].astype(F32)).astype(BF)
                x_copy(k, dx, x).start()
            half[k, x] = half[k, x] + sib_in[k, x].astype(F32)

        def token_rows(ref, k):
            return jnp.concatenate(
                [ref[pl.ds(j * local + row(k), rows), :].astype(F32) for j in range(4)], axis=0
            )

        def z_copy(k, dz):
            src = stat_z.at[k, z]
            return remote(src, src, send_sem.at[3, k], z_recv.at[k, z], at(dz=dz))

        def y_copy(k, dy):
            src = stat_y.at[k, y]
            return remote(src, src, send_sem.at[4, k], y_recv.at[k, y], at(dy=dy))

        lane = lax.broadcasted_iota(jnp.int32, (four, 128), 1)

        def stats(k):
            total = half[k, x]
            for dx in (1, 3, 2):
                there = (x + dx) % 4
                x_copy(k, dx, there).wait_recv()
                total = total + x_in[k, there].astype(F32)
            o = total[:, :cols] + token_rows(res, k)
            t = total[:, cols:]
            g = gain[...]
            gy = token_rows(tar, k) * g
            o_s[k] = o
            t_s[k] = t
            g2o = g * g * o
            packed = jnp.zeros((four, 128), F32)
            for n, term in enumerate((o * o, g2o * o, gy * o, o * t, g2o * t, gy * t)):
                packed = jnp.where(lane == n, jnp.sum(term, axis=1, keepdims=True), packed)
            stat_z[k, z] = packed.T[:8]
            for dz in (4, 3, 5, 2, 6, 1, 7):
                z_copy(k, dz).start()

        def stats_y(k):
            for dz in range(1, NZ):
                there = zs[dz]
                ref = stat_z.at[k, there]
                remote(ref, ref, send_sem.at[3, k], z_recv.at[k, there], sibling).wait_recv()
            stat_y[k, y] = jnp.sum(stat_z[k], axis=0)
            for dy in (2, 1, 3):
                y_copy(k, dy).start()

        def rows_copy(k, cc, xx, sem, to):
            ref = rows_s.at[k, cc * 4 + xx]
            return remote(ref, ref, send_sem.at[5, k], rows_recv.at[k, sem], to)

        def hessian(k):
            for dy in range(1, NY):
                there = ys[dy]
                ref = stat_y.at[k, there]
                remote(ref, ref, send_sem.at[4, k], y_recv.at[k, there], sibling).wait_recv()
            sums = jnp.sum(stat_y[k], axis=0)
            s_oo, s_goo, s_yo, s_ot, s_got, s_yt = (sums[n : n + 1] for n in range(6))
            inv = 1.0 / jnp.sqrt(s_oo / D + EPSILON)
            stretch = s_ot * inv / D
            centre = (s_goo * inv - s_yo) * inv / D
            tilt = stretch * inv
            centre_dot = (2.0 * inv * s_got - s_yt + tilt * (s_yo - 2.0 * inv * s_goo)) * inv / D
            k1 = inv * inv / tokens
            coef = jnp.concatenate(
                [centre, k1, -2.0 * tilt * k1, -centre_dot * k1, tilt * inv / tokens]
                + [jnp.zeros((123, four), F32)],
                axis=0,
            ).T
            o, t, g = o_s[k], t_s[k], gain[...]
            gy = token_rows(tar, k) * g
            out = (g * g - coef[:, 0:1]) * (t * coef[:, 1:2] + o * coef[:, 2:3])
            out = out + o * coef[:, 3:4] + gy * coef[:, 4:5]
            rows_s[k, core * 4 + x] = out.astype(BF)
            for dx in (2, 1, 3):
                rows_copy(k, core, x, x, at_x(dx)).start()
            rows_copy(k, core, x, 4 + x, sibling).start()

        def share(k):
            for dx in (1, 3, 2):
                there = (x + dx) % 4
                rows_copy(k, core, there, there, sibling).wait_recv()
                rows_copy(k, core, there, 4 + there, sibling).start()

        def backward(k):
            for xx in range(4):
                rows_copy(k, 1 - core, xx, 4 + xx, sibling).wait_recv()
            rhs = rows_s[k].reshape(n_blocks * rows, cols)

            def tile(i, carry):
                at_cols = pl.ds(pl.multiple_of(i * 256, 256), 256)
                lhs = hid[:, span(k), at_cols].reshape(n_blocks * rows, 256)
                prod[at_cols, :] += lax.dot_general(
                    lhs, rhs, (((0,), (0,)), ((), ())), preferred_element_type=F32
                )
                return carry

            lax.fori_loop(0, ff // 256, tile, 0)

        def drain(k):
            sent(hid.at[pl.ds(0, n_blocks - 1), span(k)], send_sem.at[0, k])
            sent(sib_out.at[k], send_sem.at[1, k])
            sent(x_out.at[k, pl.ds(0, 3)], send_sem.at[2, k])
            sent(stat_z.at[k, pl.ds(0, 7)], send_sem.at[3, k])
            sent(stat_y.at[k, pl.ds(0, 3)], send_sem.at[4, k])
            sent(rows_s.at[k, pl.ds(0, 7)], send_sem.at[5, k])

        return dict(forward=forward, pair=pair, stats=stats, stats_y=stats_y, hessian=hessian,
                    share=share, backward=backward, wave=wave, drain=drain)

    def prepare():
        for load in loads[1:]:
            load.wait()
        vb[...] = vc[...].astype(BF)
        prod[...] = -beta_prev[0] * vp[...]
        v_sq[0] = jnp.sum(vc[...] * vc[...])

    groups, n_stages = [], 0
    for n, (first, rows, stages) in enumerate(GROUPS):
        refs = of_groups[n * REFS : (n + 1) * REFS]
        groups.append((n_stages, stages, steps_of(first, rows, *refs)))
        n_stages += stages

    loads[0].wait()
    groups[0][2]["wave"](0, 0)

    def body(i, carry):
        for op, lag in SCHEDULE:
            if op == "prepare":
                pl.when(i == lag)(prepare)
                continue
            for base, stages, steps in groups:
                k = i - lag - base

                @pl.when((k >= 0) & (k < stages))
                def _(op=op, k=k, steps=steps):
                    if isinstance(op, int):
                        steps["wave"](op, k)
                    else:
                        steps[op](k)

        return carry

    lax.fori_loop(0, n_stages + max(lag for _, lag in SCHEDULE), body, 0)

    out_copy = pltpu.make_async_copy(prod, update, local_sem.at[6])
    out_copy.start()
    u, v = prod[...], vc[...]
    along = jnp.sum(u * v)
    own = along / jnp.maximum(v_sq[0], 1e-30)
    left = u - own * v
    lanes = lax.broadcasted_iota(jnp.int32, (8, 128), 1)

    def pack(values):
        packed = jnp.zeros((8, 128), F32)
        for n, value in enumerate(values):
            packed = jnp.where(lanes == n, value, packed)
        return packed

    def merge(ref):
        facts = ref[:, 0, :]
        square, along, own, left, rest = (facts[:, n : n + 1] for n in range(5))

        def total(part):
            return jnp.sum(part, axis=0, keepdims=True)

        all_square, all_along = total(square), total(along)
        joint = all_along / jnp.maximum(all_square, 1e-30)
        shift = own - joint
        return (
            all_square, all_along, joint,
            total(left + shift * (shift * square + 2.0 * rest)), total(rest + shift * square),
        )

    def fact_copy(level, ref, n, to):
        return remote(ref, ref, fact_send.at[level], fact_recv.at[level, n], to)

    fact_fs[fs] = pack((v_sq[0], along, own, jnp.sum(left * left), jnp.sum(left * v)))
    for dy, dz in others:
        fact_copy(0, fact_fs.at[fs], fs, at(dy, dz)).start()
    for dy, dz in reversed(others):
        there = ys[dy] * NZ + zs[dz]
        fact_copy(0, fact_fs.at[there], there, sibling).wait_recv()
    fact_t[tp] = pack(merge(fact_fs))
    for d in (4, 5, 3, 2, 6, 7, 1):
        fact_copy(1, fact_t.at[tp], tp, (fs, (tp + d) % NT)).start()
    for d in range(1, NT):
        there = (tp + d) % NT
        fact_copy(1, fact_t.at[there], there, sibling).wait_recv()
    scale = 1.0 / (FF * D)
    total, along, joint, left, rest = merge(fact_t)
    alpha = along * scale
    shift = joint - alpha
    square = left + shift * (shift * total + 2.0 * rest)
    beta = jnp.sqrt(square * scale)
    facts_out[...] = jnp.where(lanes == 0, alpha, beta)

    out_copy.wait()
    for _, stages, steps in groups:
        for k in range(stages):
            steps["drain"](k)
    sent(fact_fs.at[pl.ds(0, n_blocks - 1)], fact_send.at[0])
    sent(fact_t.at[pl.ds(0, NT - 1)], fact_send.at[1])


def finish(update, v_cur, facts, out, alpha_out, beta_out):
    alpha, beta = facts[0:1, 0:1], facts[0:1, 1:2]
    out[...] = (update[...] - alpha * v_cur[...]) / beta

    @pl.when(pl.program_id(0) == 0)
    def _():
        alpha_out[0, 0] = facts[0, 0]
        beta_out[0, 0] = facts[0, 1]


def on_device(hidden, residual, target, norm_gain, weight, v_prev, v_cur, beta_prev):
    tokens, ff = hidden.shape
    cols = weight.shape[1]
    blocks = NY * NZ
    _, slots = gather_plan(ff)
    dma = pltpu.SemaphoreType.DMA
    anywhere, vmem = pl.BlockSpec(memory_space=pl.ANY), pl.BlockSpec(memory_space=pltpu.VMEM)
    scratch = [
        pltpu.VMEM((blocks, tokens, ff), BF),
        pltpu.VMEM((ff, cols), BF),
        pltpu.VMEM((ff, cols), BF),
        pltpu.VMEM((ff, cols), F32),
        pltpu.VMEM((ff, cols), F32),
        pltpu.VMEM(residual.shape, BF),
        pltpu.VMEM(target.shape, BF),
        pltpu.VMEM((ff, cols), F32),
        pltpu.VMEM((blocks, 8, 128), F32),
        pltpu.VMEM((NT, 8, 128), F32),
        pltpu.SMEM((1,), F32),
        dma((7,)),
        dma((2, blocks)),
        dma((2,)),
    ]
    for _, rows, stages in GROUPS:
        four = 4 * rows
        scratch += [
            pltpu.VMEM((stages, 4, four, 2 * cols), BF),
            pltpu.VMEM((stages, 4, four, 2 * cols), BF),
            pltpu.VMEM((stages, 4, four, 2 * cols), F32),
            pltpu.VMEM((stages, 4, four, 2 * cols), BF),
            pltpu.VMEM((stages, 4, four, 2 * cols), BF),
            pltpu.VMEM((stages, four, cols), F32),
            pltpu.VMEM((stages, four, cols), F32),
            pltpu.VMEM((stages, NZ, 8, four), F32),
            pltpu.VMEM((stages, NY, 8, four), F32),
            pltpu.VMEM((stages, 8, four, cols), BF),
            dma((stages, slots)),
            dma((stages,)),
            dma((stages, 4)),
            dma((stages, NZ)),
            dma((stages, NY)),
            dma((stages, 8)),
            dma((6, stages)),
        ]
    update, facts = pl.pallas_call(
        kernel,
        out_shape=(jax.ShapeDtypeStruct((ff, cols), F32), jax.ShapeDtypeStruct((8, 128), F32)),
        in_specs=[anywhere] * 3 + [vmem] + [anywhere] * 3 + [pl.BlockSpec(memory_space=pltpu.SMEM)],
        out_specs=(anywhere, vmem),
        scratch_shapes=scratch,
        compiler_params=pltpu.CompilerParams(
            collective_id=0, has_side_effects=True, vmem_limit_bytes=60 << 20
        ),
    )(
        hidden, residual, target, norm_gain.reshape(1, cols), weight, v_prev, v_cur,
        beta_prev.reshape(1),
    )
    strip = pl.BlockSpec((ff // 4, cols), lambda i: (i, 0))
    scalar = pl.BlockSpec(memory_space=pltpu.SMEM)
    one = jax.ShapeDtypeStruct((1, 1), F32)
    v_next, alpha, beta = pl.pallas_call(
        finish,
        out_shape=(jax.ShapeDtypeStruct((ff, cols), F32), one, one),
        grid=(4,),
        in_specs=[strip, strip, pl.BlockSpec((8, 128), lambda i: (0, 0))],
        out_specs=(strip, scalar, scalar),
    )(update, v_cur, facts)
    return v_next, alpha.reshape(()), beta.reshape(())


def solution(mesh):
    return jax.shard_map(
        on_device,
        mesh=mesh,
        in_specs=(
            P("fsdp", "tp"),
            P("tp", "fsdp"),
            P("tp", "fsdp"),
            P("fsdp"),
            P("tp", "fsdp"),
            P("tp", "fsdp"),
            P("tp", "fsdp"),
            P(),
        ),
        out_specs=(P("tp", "fsdp"), P(), P()),
        check_vma=False,
    )
```

time: 631 us -> 149 us (0.24)
  blocking collectives: 325 us -> 0 us
  waiting for transfers between devices: 243 us -> 0 us
  Pallas kernels: 0 us -> 147 us
  matrix products: 25.2 us -> 0 us
  between operations: 18.1 us -> 1.29 us
  other arithmetic: 11.2 us -> 0 us
  local copies, waits for them, and re-layouts: 8.43 us -> 0 us
    psum x5 -> x0, blocking collectives: 325 us -> none  [the longest x1 76.7 us: on_device(): alpha = lax.psum(jnp.sum(update * v_cur), ('fsdp', 'tp')) * scale]
    all_gather x2 -> x0, waiting for transfers between devices: 191 us -> none  [the longest x1 135 us: on_device(): gathered = lax.all_gather(hidden, 'fsdp', axis=0, tiled=True)]
    pallas_call x0 -> x2, Pallas kernels: none -> 147 us  [the longest x1 143 us: on_device(): pl.pallas_call(kernel, out_shape=(jax.ShapeDtypeStruct((ff, cols), F32),...]
    reduce_scatter x1 -> x0, waiting for transfers between devices: 50.7 us -> none  [on_device(): lax.psum_scatter(jnp.dot(block_rows, stacked, preferred_element_type=jnp....]
    dot_general x2 -> x0, matrix products: 25.2 us -> none  [the longest x1 13.1 us: on_device(): jnp.dot(block_rows, stacked, preferred_element_type=jnp.float32)]
    unnamed x15 -> x0, local copies, waits for them, and re-layouts: 8.43 us -> none
  transfers between devices with their start and end apart: 3 -> 0, of which waited for: 3 -> 0; matrix products, arithmetic and copies ran while one was open for 1% -> 0% of each run, Pallas kernels for 0% -> 0%
where the time goes in v3:
time: 149 us
  Pallas kernels  147 us (99%)
    pallas_call x1, Pallas kernels, on_device(): pl.pallas_call(kernel, out_shape=(jax.ShapeDtypeStruct((ff, cols), F32),...  143 us
    pallas_call x1, Pallas kernels, on_device(): pl.pallas_call(finish, out_shape=(jax.ShapeDtypeStruct((ff, cols), F32),...  4.34 us

profile of v3, /device:TPU:1, one launch (start us, length us, event | category | flops | bytes accessed | tf_op | source)
XLA Modules:
  0.0 148.6 jit_solution(16361026964548491284)
XLA Ops:
  1.3 143.0 %shard_map.103 = (f32[1792,256]{1,0:T(8,128)}, f32[8,128]{1,0:T(8,128)}) custom-call(bf16[128,1792]{1,0:T(8,128)(2,1)} %hidden.1, bf16[512,256]{1,0:T(8,128)(2,1)} %residual.1, bf16[512,256]{1,0:T(8,128)(2,1)} %target.1, f32[1,256]{1,0:T(1,128)} %bitcast.5, bf16[1792,256]{1,0:T(8,128)(2,1)} %weight.1, f32[1792,256]{1,0:T(8,128)} %v_prev.1, ...), custom_call_target="tpu_custom_call" | custom-call | tf_op jit(solution)/shard_map/pallas_call | solution.py:462
  144.3 4.3 %shard_map.104 = (f32[1792,256]{1,0:T(8,128)}, f32[1,1]{1,0:T(1,128)}, f32[1,1]{1,0:T(1,128)}) custom-call(f32[1792,256]{1,0:T(8,128)} %get-tuple-element.8.update, f32[1792,256]{1,0:T(8,128)} %v_cur.3, f32[8,128]{1,0:T(8,128)} %get-tuple-element.9.facts), custom_call_target="tpu_custom_call" | custom-call | tf_op jit(solution)/shard_map/pallas_call | solution.py:478

commit v4 on v3

--- a/solution.py
+++ b/solution.py
@@ -15,8 +15,8 @@
 GROUPS = ((0, 32, 3), (96, 16, 2))
 SPLIT = 1024
 SCHEDULE = [
-    ("prepare", 1), ("pair", 3), ("stats", 4), ("stats_y", 5), ("hessian", 6), ("share", 7),
-    ("backward", 8), (0, -1), (1, 0), (3, 1), (5, 2), (2, 0), (4, 1), (6, 2), ("forward", 2),
+    ("pair", 3), ("stats", 4), ("stats_y", 5), ("hessian", 6), ("share", 7), ("backward", 8),
+    (0, -1), ("prepare", 0), (1, 0), (3, 1), (5, 2), (2, 0), (4, 1), (6, 2), ("forward", 2),
 ]
 REFS = 17
 BF, F32 = jnp.bfloat16, jnp.float32

time: 149 us -> 149 us (level)
  no operation moved by 1% of the time
where the time goes in v4:
time: 149 us
  Pallas kernels  147 us (99%)
    pallas_call x1, Pallas kernels, on_device(): pl.pallas_call(kernel, out_shape=(jax.ShapeDtypeStruct((ff, cols), F32),...  143 us
    pallas_call x1, Pallas kernels, on_device(): pl.pallas_call(finish, out_shape=(jax.ShapeDtypeStruct((ff, cols), F32),...  4.34 us

profile of v4, /device:TPU:1, one launch (start us, length us, event | category | flops | bytes accessed | tf_op | source)
XLA Modules:
  0.0 148.6 jit_solution(6071943027710444305)
XLA Ops:
  1.3 143.0 %shard_map.103 = (f32[1792,256]{1,0:T(8,128)}, f32[8,128]{1,0:T(8,128)}) custom-call(bf16[128,1792]{1,0:T(8,128)(2,1)} %hidden.1, bf16[512,256]{1,0:T(8,128)(2,1)} %residual.1, bf16[512,256]{1,0:T(8,128)(2,1)} %target.1, f32[1,256]{1,0:T(1,128)} %bitcast.5, bf16[1792,256]{1,0:T(8,128)(2,1)} %weight.1, f32[1792,256]{1,0:T(8,128)} %v_prev.1, ...), custom_call_target="tpu_custom_call" | custom-call | tf_op jit(solution)/shard_map/pallas_call | solution.py:462
  144.3 4.3 %shard_map.104 = (f32[1792,256]{1,0:T(8,128)}, f32[1,1]{1,0:T(1,128)}, f32[1,1]{1,0:T(1,128)}) custom-call(f32[1792,256]{1,0:T(8,128)} %get-tuple-element.8.update, f32[1792,256]{1,0:T(8,128)} %v_cur.3, f32[8,128]{1,0:T(8,128)} %get-tuple-element.9.facts), custom_call_target="tpu_custom_call" | custom-call | tf_op jit(solution)/shard_map/pallas_call | solution.py:478
